TPU v7x, 256 devices: a whole 4x4x8 slice. The times are simulated.
256 devices in a mesh: space: 64 (over x_hi, y, z), tm: 4 (over x_lo, core).
Axes of the slice: x: 4 (x_hi: 2, x_lo: 2; x = x_hi * 2 + x_lo), y: 4, z: 8, core: 2. Of those that a mesh axis runs over, the one named last changes fastest.
Arguments:
- field: float32 [10, 16, 256, 128, 128], P(None, 'tm', 'space'), may hold values from -6 to 6
Outputs:
- spectrum: float32 [2, 10, 16, 1024, 32], P(None, None, 'tm', 'space')
All inputs are finite; a program needn't handle non-finite values.
Results may differ from a plain program's by a relative error of at most 0.00007.
Values sent between devices are 32-bit elements; how exact they have to be, the bound alone decides.
A program may use at most 128 MiB of HBM per device.

v0:
```python
import functools
import math

import jax
import jax.numpy as jnp
import ml_dtypes
import numpy as np
from jax import lax
from jax.experimental import pallas as pl
from jax.experimental.pallas import tpu as pltpu
from jax.sharding import PartitionSpec as P

MESH = pl.DeviceIdType.MESH
BF = jnp.bfloat16
F32 = jnp.float32

CH = 10
NX = 128
NY = 128
NT = 16
NZ = 256
SPACE = 64
TM = 4
GROUPS = ((0, 4), (4, 4), (8, 2))
STEP = 24
MOVES = ((0, 1), (1, 3))
OFFSETS = sorted(
    [(k // 32, (k // 8) % 4, k % 8) for k in range(1, SPACE)],
    key=lambda at: (-2 * at[0] - min(at[1], 4 - at[1]) - min(at[2], 8 - at[2]), at[1], at[2]),
)
PLANE_OFFSETS = [(1, 2), (1, 1), (1, 3), (1, 0), (0, 2), (0, 1), (0, 3), (0, 0)]
TIME_AT = (0, 32, 64, 80)


def halves(table):
    high = table.astype(ml_dtypes.bfloat16)
    low = (table - high.astype(np.float64)).astype(ml_dtypes.bfloat16)
    return high, low


def angle(freq, pos, length):
    return 2.0 * math.pi * ((freq * pos) % length) / length


def real_modes(order):
    cells = np.arange(128)
    rows = np.zeros((40, 128))
    for e in range(16):
        rows[order(e, 0)] = np.cos(angle(e, cells, 128))
        rows[order(e, 1)] = np.sin(angle(e, cells, 128)) if e else np.cos(angle(16, cells, 128))
    rows[32] = np.sin(angle(16, cells, 128))
    return rows


def plane_tables():
    def build(order):
        high, low = halves(real_modes(order))
        return np.concatenate([np.concatenate([high, high], 1), np.concatenate([low, low], 1)], 0)

    wx = build(lambda e, c: 2 * e + c)
    up = build(lambda e, c: 16 * c + e)
    down = build(lambda e, c: 16 * c + (16 - e) % 16)
    return wx, np.stack([up, down])


def depth_tables():
    depth = np.arange(NZ)
    k = np.arange(32)[:, None]
    both = np.concatenate([np.cos(angle(k, depth, NZ)), np.sin(angle(k, depth, NZ))], 0)
    main = np.zeros((2, 64, SPACE, 2, 4))
    for c in range(2):
        main[c, :, :, c, :] = both.reshape(64, SPACE, 4)
    main = main.reshape(128, 512)
    main2 = main.reshape(-1, SPACE, 2, 2, 2).transpose(0, 3, 1, 2, 4).reshape(-1, 512)
    both2 = both.reshape(-1, SPACE, 2, 2).transpose(0, 2, 1, 3).reshape(-1, 256)
    return [np.concatenate(halves(table), 0) for table in (main, main2, both, both2)]


def time_tables():
    def phase(q, step):
        return np.exp(-1j * angle(q if q < 8 else q - 16, step, NT))

    def pack(table, pad):
        high, low = halves(table)
        blank = np.zeros(table.shape[:-1] + (pad,), ml_dtypes.bfloat16)
        return np.concatenate([np.concatenate([part, part, blank], -1) for part in (high, low)], -2)

    out = []
    for count in (4, 2):
        table = np.zeros((2, 2, 2, 2, TM, 8, TM, 2, count, 4))
        for n in range(count):
            half, rest = divmod(n, count // 2)
            for q in range(16):
                for step in range(16):
                    value = phase(q, step)
                    for sx, sign in ((0, 1), (1, -1)):
                        at = (sx, q // 4, (q % 4) * 2 + rest, step // 4)
                        for zero in range(2):
                            if zero:
                                terms = ((sx, value),)
                            else:
                                terms = ((0, value), (1, -1j * sign * value))
                            for c, term in terms:
                                table[(zero, half, 0) + at + (c, n, step % 4)] = term.real
                                table[(zero, half, 1) + at + (c, n, step % 4)] = term.imag
        out.append(pack(table.reshape(2, 256, 32 * count), 0))
    table = np.zeros((3, 2, 2, TM, 8, TM, CH, 4))
    for n in range(CH):
        ng = n // 4
        half, rest = divmod(n % 4, 2) if ng < 2 else (n - 8, 0)
        for q in range(16):
            for step in range(16):
                term = 1j * phase(q, step)
                at = (q // 4, (q % 4) * 2 + rest, step // 4, n, step % 4)
                table[(ng, half, 0) + at] = term.real
                table[(ng, half, 1) + at] = term.imag
    out.append(pack(table.reshape(384, 160), 64))
    return out


def lane_tables():
    scale = 1.0 / math.sqrt(NX * NY * NZ * NT)
    out = np.zeros((3, 2, 2, 128, 2, 2, 2, 32))
    for sy, sign in ((0, 1), (1, -1)):
        for k in range(32):
            for kind in range(3):
                coef = np.zeros(128, complex)
                if kind == 0:
                    coef[k], coef[32 + k] = 1, -1j
                    coef[64 + k], coef[96 + k] = -1j * sign, -sign
                elif kind == 1:
                    at = 64 * sy
                    coef[at + k], coef[at + 32 + k] = 1, -1j
                elif sy == 1:
                    coef[k], coef[32 + k] = 1j, 1
                for w in range(2):
                    out[kind, w, 0, :, sy, w, 0, k] = coef.real
                    out[kind, w, 1, :, sy, w, 0, k] = -coef.imag
                    out[kind, w, 0, :, sy, w, 1, k] = coef.imag
                    out[kind, w, 1, :, sy, w, 1, k] = coef.real
    return (out.reshape(3, 512, 256) * scale).astype(ml_dtypes.bfloat16)


def all_tables():
    wx, wy = plane_tables()
    wz, wz2, wzb, wzb2 = depth_tables()
    m01, m2, mx = time_tables()
    pieces = {
        "wx": wx, "wy": wy.reshape(160, 256), "m01": m01.reshape(1024, 256), "m2": np.concatenate([m2[0], m2[1]], 1),
        "lanes": lane_tables().reshape(1536, 256), "wzb": wzb, "wzb2": wzb2,
    }
    for name, table in (("wz", wz), ("wz2", wz2), ("mx", mx)):
        wide = np.concatenate([table, np.zeros((len(table), -table.shape[1] % 256), ml_dtypes.bfloat16)], 1)
        pieces[name] = np.concatenate([wide[:, :256], wide[:, 256:]], 0)
    first, at = {}, 0
    for name, table in pieces.items():
        first[name] = at
        at += len(table)
    return np.concatenate(list(pieces.values()), 0), first


def split(values):
    high = values.astype(BF)
    return high, (values - high.astype(F32)).astype(BF)


def dot(a, b):
    return jnp.dot(a, b, preferred_element_type=F32)


def owner(g, u):
    return jnp.where(u < 2, 2 * g + u, jnp.where(g == 0, 32, 64 - 2 * g) + u - 2)


def place(s):
    b, h = s // 2, s % 2
    g = jnp.where(b < 16, b, jnp.where(b == 16, 0, 32 - b))
    return g, jnp.where(b < 16, h, 2 + h)


def kernel(
    at_of, field, tables, out,
    planes, rows, rows_x, wx, wy, wz, wz2, wzb, wzb2, m01, m2, mx, lanes, lanes_b,
    send_a, send_b, recv_a, recv_b, time_send, time_send_x, time_sb, time_sbx,
    time_recv, time_recv_x, time_rb, time_rbx, sorts, last, blocks,
    field_sem, const_sem, ssa, rsa, ssx, rsx, ssb, rsb, sst, rst, sstx, rstx, sstb, rstb, sstbx, rstbx, ssl, rsl,
):
    s, tm = lax.axis_index("space"), lax.axis_index("tm")
    g, u = place(s)
    e = 4 * u + tm
    zero_g, zero_e, zero_u = g == 0, e == 0, u == 0
    pick_e, pick_g = jnp.where(zero_e, 1, 0), jnp.where(zero_g, 1, 0)

    def field_copy(pair):
        two = pl.ds(2 * pair, 2)
        return pltpu.make_async_copy(field.at[two], planes.at[two], field_sem.at[pair])

    def table_copy(i, dst, name, skip=0, columns=slice(None)):
        rows_at = pl.ds(pl.multiple_of(at_of[name] + skip, 16), dst.shape[0])
        return pltpu.make_async_copy(tables.at[rows_at, columns], dst, const_sem.at[i])

    consts = [
        table_copy(0, wx, "wx"),
        table_copy(1, wy, "wy"),
        table_copy(2, wz.at[:, :256], "wz"),
        table_copy(3, wz.at[:, 256:], "wz", 256),
        table_copy(4, wzb, "wzb"),
        table_copy(5, wzb2, "wzb2"),
        table_copy(6, m01, "m01", 512 * pick_e),
        table_copy(7, m2, "m2", 0, pl.ds(pl.multiple_of(128 * pick_e, 128), 128)),
        table_copy(8, mx.at[:, :256], "mx"),
        table_copy(9, mx.at[:, 256:], "mx", 768, slice(0, 128)),
        table_copy(10, lanes, "lanes", 512 * pick_g),
        table_copy(11, lanes_b, "lanes", 1024),
        table_copy(12, wz2.at[:, :256], "wz2"),
        table_copy(13, wz2.at[:, 256:], "wz2", 256),
    ]
    consts[0].start()
    field_copy(0).start()
    consts[1].start()

    barrier = pltpu.get_barrier_semaphore()

    def greet(space, time):
        pl.semaphore_signal(barrier, inc=1, device_id={"space": space, "tm": time}, device_id_type=MESH)


    def turn(value, count):
        return jnp.where(value >= count, value - count, value)

    place_x, place_y, place_z = s // 32, (s // 8) % 4, s % 8
    along = (
        [32 * turn(place_x + d, 2) for d in range(2)],
        [8 * turn(place_y + d, 4) for d in range(4)],
        [turn(place_z + d, 8) for d in range(8)],
    )
    round_z = turn(place_z, 6)
    z_order = [turn(turn(round_z + i, 6) + 6, 8) for i in range(6)] + [4 + turn(place_z % 2 + i, 2) for i in range(2)]
    others = [along[0][x] + along[1][y] + along[2][z] for x, y, z in OFFSETS]
    for to in others:
        greet(to, tm)

    for j in range(1, TM):
        greet(s, turn(tm + j, TM))
        for v in range(1, 4):
            greet(owner(g, turn(u + v, 4)), turn(tm + j, TM))

    for pair in range(1, CH // 2):
        field_copy(pair).start()
    for copy in consts[2:]:
        copy.start()

    rows_x[...] = jnp.zeros_like(rows_x)
    send_b[...] = jnp.zeros_like(send_b)

    def plane_step(ng, first, n):
        products = []
        for t in range(4):
            for pair in range(2):
                high, low = split(jnp.concatenate([planes[n, t, 2 * pair], planes[n, t, 2 * pair + 1]], axis=1))
                both = dot(wx[...], jnp.concatenate([high, low], axis=0))
                products.append((t, pair, both[:40] + both[40:]))
        for t, pair, both in products:
            at = pl.multiple_of(((n - first) * 4 + t) * 8, 8)
            for half in range(2):
                z = 2 * pair + half
                part = both[:, 128 * half : 128 * half + 128]
                for v in range(4):
                    tile = part[8 * v : 8 * v + 8]
                    if ng < 2:
                        rows[ng, z, pl.ds(v * 128 + at, 8), :] = tile
                    else:
                        rows[2, half, pl.ds(v * 128 + pair * 64 + at, 8), :] = tile
                rows_x[half, pl.ds(64 * pair + 4 * n + t, 1), :] = part[32:33]

    def along_y(values, side):
        high, low = split(values)
        both = lax.dot_general(
            wy[80 * side : 80 * side + 80, :], jnp.concatenate([high, low], axis=1), (((1,), (1,)), ((), ())),
            preferred_element_type=F32,
        )
        return both[:40] + both[40:]

    def exchange(ng):
        count = 4 if ng < 2 else 2
        products = [
            (z, side, along_y(rows[ng, z, 256 * side : 256 * side + 256, :], side)) for z in range(count) for side in range(2)
        ]
        extras = [along_y(rows_x[z], 0) for z in range(2)] if ng == 2 else []
        for z, side, both in products:
            for h in range(2):
                lanes_h = slice(128 * h, 128 * h + 128)
                for c in range(2):
                    at = (side * 32 + h) * STEP + 8 * ng + count * c + z
                    send_a[pl.ds(at, 16, stride=2 * STEP), :] = both[16 * c : 16 * c + 16, lanes_h]
                send_b[pl.ds((2 * side + h) * 12 + 4 * ng + z, 1), :] = both[32:33, lanes_h]
        for z, both in enumerate(extras):
            for c in range(2):
                send_a[pl.ds(20 + 2 * c + z, 16, stride=2 * STEP), :] = both[16 * c : 16 * c + 16]
            send_b[pl.ds(10 + z, 1), :] = both[32:33]

    def sent(move):
        first, end = MOVES[move]
        return 8 * first, 8 * (end - first) - (4 if end == 3 else 0)

    def sent_b(move):
        first, end = MOVES[move]
        return 4 * first, 4 * (end - first)

    def remote(src, dst, send_sem, recv_sem, space, time):
        return pltpu.make_async_remote_copy(
            src_ref=src, dst_ref=dst, send_sem=send_sem, recv_sem=recv_sem,
            device_id={"space": space, "tm": time}, device_id_type=MESH,
        )

    def space_copy(move, to):
        first, count = sent(move)
        src = pl.ds(pl.multiple_of(to * STEP + first, 8), count)
        return remote(send_a.at[src], recv_a.at[s, pl.ds(first, count)], ssa.at[move], rsa.at[move], to, tm)

    def send_space(move):
        first, count = sent(move)
        here = (s, pl.ds(first, count))
        last_move = move == len(MOVES) - 1

        for z in z_order:
            for x, y in PLANE_OFFSETS:
                to = along[0][x] + along[1][y] + z
                if x or y:
                    space_copy(move, to).start()
                else:
                    @pl.when(to != s)
                    def _():
                        space_copy(move, to).start()

        if last_move:
            here_x = (s, pl.ds(20, 4))

            @pl.loop(0, 16)
            def _(k):
                @pl.when(2 * k != s)
                def _():
                    src = pl.ds(pl.multiple_of(2 * k * STEP + 20, 4), 4)
                    remote(send_a.at[src], recv_a.at[here_x], ssx.at[0], rsx.at[0], 2 * k, tm).start()

            @pl.when(zero_u)
            def _():
                recv_a[here_x] = send_a[pl.ds(pl.multiple_of(s * STEP + 20, 4), 4), :]

        first_b, count_b = sent_b(move)
        here_b = (s, pl.ds(first_b, count_b))
        for v, to in enumerate((0, 1, 32, 33)):
            src = pl.ds(12 * v + first_b, count_b)

            @pl.when(s != to)
            def _():
                remote(send_b.at[src], recv_b.at[here_b], ssb.at[move], rsb.at[move], to, tm).start()

            @pl.when(s == to)
            def _():
                recv_b[here_b] = send_b[src, :]

        recv_a[here] = send_a[pl.ds(pl.multiple_of(s * STEP + first, 8), count), :]

    consts[0].wait()
    for ng, (first, count) in enumerate(GROUPS):
        @pl.loop(first, first + count, step=2)
        def _(n):
            field_copy(n // 2).wait()
            plane_step(ng, first, n)
            plane_step(ng, first, n + 1)

        if ng == 0:
            consts[1].wait()
        exchange(ng)
        if ng == 0:
            pl.semaphore_wait(barrier, 63 + 3 + 9)
        for move, (_, end) in enumerate(MOVES):
            if ng == end - 1:
                send_space(move)

    for copy in consts[2:]:
        copy.wait()

    def wait_rows(rows_of, count, sem):
        pltpu.make_async_copy(rows_of.at[pl.ds(0, count)], rows_of.at[pl.ds(0, count)], sem).wait()

    def moved(ng):
        return TIME_AT[ng], TIME_AT[ng + 1] - TIME_AT[ng]

    def keep_time(ng, sort, z_rows, src, src_x):
        count = (TIME_AT[ng + 1] - TIME_AT[ng]) // 2
        sort[...] = z_rows
        for v in range(TM):
            for c in range(2):
                at = 80 * v + TIME_AT[ng] + count * c
                src[at : at + count, :] = sort[pl.ds(2 * v + c, count, stride=8), :]
        if ng == 2:
            src_x[...] = z_rows[64:104]

    def send_time(ng, src, src_x, dst, dst_x, send_sem, recv_sem, send_sem_x, recv_sem_x):
        first, count = moved(ng)
        mine = pl.ds(pl.multiple_of(tm * 80 + first, 8), count)
        here = (tm, pl.ds(first, count))
        for j in range(1, TM):
            to = tm + j
            to = jnp.where(to >= TM, to - TM, to)
            there = pl.ds(pl.multiple_of(to * 80 + first, 8), count)
            remote(src.at[there], dst.at[here], send_sem.at[ng], recv_sem.at[ng], s, to).start()
        dst[here] = src[mine, :]
        if ng == 2:
            at_x = pl.ds(pl.multiple_of(tm * 40, 8), 40)

            @pl.when(jnp.logical_and(zero_u, tm != 0))
            def _():
                remote(src_x, dst_x.at[at_x], send_sem_x.at[0], recv_sem_x.at[0], s, 0).start()

            @pl.when(zero_e)
            def _():
                dst_x[pl.ds(0, 40), :] = src_x[...]

    time_a = (time_send, time_send_x, time_recv, time_recv_x, sst, rst, sstx, rstx)
    time_b = (time_sb, time_sbx, time_rb, time_rbx, sstb, rstb, sstbx, rstbx)

    def received(ref, ng):
        size = ref.shape[1] // 3
        count = SPACE * size
        values = ref[:, size * ng : size * ng + size, :].reshape(count, 128) if ng < 2 else None
        if ng == 2:
            count //= 2
            main, extra = (
                ref[:, at : at + size // 2, :].reshape(count, 128) for at in (2 * size, 2 * size + size // 2)
            )
            lower = lax.broadcasted_iota(jnp.int32, (count, 128), 1) < 64
            values = jnp.concatenate(
                [jnp.where(lower, main, pltpu.roll(extra, 64, 1)), jnp.where(lower, pltpu.roll(main, 64, 1), extra)], axis=0
            )
        high, low = split(values)
        return jnp.concatenate([high, low], axis=1)

    def depth_step(move):
        first, end = MOVES[move]
        wait_rows(send_a, 63 * sent(move)[1], rsa.at[move])
        if end == 3:
            @pl.when(zero_u)
            def _():
                wait_rows(send_a, 63 * 4, rsx.at[0])

        for ng in range(first, end):
            both = dot(wz[...] if ng < 2 else wz2[...], received(recv_a, ng))
            keep_time(ng, sorts.at[ng], (both[:128, :128] + both[:128, 128:] + both[128:, :128]).T, *time_a[:2])
            send_time(ng, *time_a)

        @pl.when(zero_g)
        def _():
            wait_rows(send_a, 63 * sent_b(move)[1], rsb.at[move])
            for ng in range(first, end):
                both = dot(wzb[...] if ng < 2 else wzb2[...], received(recv_b, ng))
                z_rows = both[:64, :128] + both[:64, 128:] + both[64:, :128]
                keep_time(ng, sorts.at[3 + ng], jnp.concatenate([z_rows, jnp.zeros_like(z_rows)], axis=0).T, *time_b[:2])
                send_time(ng, *time_b)

    def finish(values, table, signs):
        high, low = split(values)
        fill = table.shape[1] - 2 * values.shape[0]
        parts = [high, low] + ([jnp.zeros((fill, 128), BF)] if fill else [])
        both = dot(table[...], jnp.concatenate(parts, axis=0))
        both = both[: both.shape[0] // 2] + both[both.shape[0] // 2 :]
        count = both.shape[0] // 4
        pairs = [split(both[count * i : count * i + count]) for i in range(4)]
        both = jnp.concatenate([jnp.concatenate([pair[i] for pair in pairs], axis=1) for i in range(2)], axis=0)
        both = dot(both, signs[...])
        return both[:count] + both[count:]

    def keep(ng, value, first, add):
        for i in range(value.shape[0] // 8):
            for sy in range(2):
                j = 8 * sy + first + i
                part = value[8 * i : 8 * i + 8, 128 * sy : 128 * sy + 128]
                at = slice(j * STEP + 8 * ng, j * STEP + 8 * ng + 8)
                last[at, :] = last[at, :] + part if add else part

    def slot_of(sx):
        return jnp.where(sx == 0, e, jnp.where(zero_e, 0, 16 - e))

    def last_copy(j, first, count):
        at = pl.ds(pl.multiple_of(slot_of((j // 4) % 2) * STEP + first, 8), count)
        src = pl.ds(pl.multiple_of(j * STEP + first, 8), count)
        return remote(last.at[src], blocks.at[at], ssl.at[0], rsl.at[0], owner(g, j // 4), j % 4)

    def steps_of(ref, ng):
        count = TIME_AT[ng + 1] - TIME_AT[ng]
        return ref[:, TIME_AT[ng] : TIME_AT[ng + 1], :].reshape(TM * count, 128)

    def time_step(ng):
        table = m01 if ng < 2 else m2
        wait_rows(time_send, 3 * moved(ng)[1], rst.at[ng])
        keep(ng, finish(steps_of(time_recv, ng), table, lanes), 0, False)
        if ng == 2:
            @pl.when(zero_e)
            def _():
                wait_rows(time_recv_x, 120, rstx.at[0])
                value = finish_x(time_recv_x, lanes)
                for i in range(3):
                    keep(i, value[32 * i : 32 * i + 32], 4, True)

        @pl.when(zero_g)
        def _():
            wait_rows(time_sb, 3 * moved(ng)[1], rstb.at[ng])
            keep(ng, finish(steps_of(time_rb, ng), table, lanes_b), 0, True)
            if ng == 2:
                @pl.when(zero_e)
                def _():
                    wait_rows(time_rbx, 120, rstbx.at[0])
                    value = finish_x(time_rbx, lanes_b)
                    for i in range(3):
                        keep(i, value[32 * i : 32 * i + 32], 4, True)

        @pl.when(jnp.logical_not(zero_e))
        def _():
            side = jnp.where(e >= 8, 8, 0)
            for k in range(8):
                last_copy(8 - side + k, 8 * ng, 8).start()
            for k in range(1, 8):
                last_copy(side + turn(e - side + k, 8), 8 * ng, 8).start()

        @pl.when(zero_e)
        def _():
            for j in (8, 9, 10, 11, 1, 2, 3):
                last_copy(j, 8 * ng, 8).start()
            if ng == 2:
                for j in (12, 13, 14, 15, 4, 5, 6, 7):
                    last_copy(j, 0, STEP).start()

        at = pl.ds(pl.multiple_of(slot_of(u % 2) * STEP + 8 * ng, 8), 8)
        blocks[at, :] = last[pl.ds(pl.multiple_of(e * STEP + 8 * ng, 8), 8), :]

    def finish_x(ref, signs):
        high, low = split(ref[...])
        both = dot(mx[...], jnp.concatenate([high, low, jnp.zeros((64, 128), BF)], axis=0))
        both = both[:384] + both[384:]
        values = []
        for i in range(3):
            pairs = [split(both[128 * i + 32 * j : 128 * i + 32 * j + 32]) for j in range(4)]
            value = jnp.concatenate([jnp.concatenate([pair[h] for pair in pairs], axis=1) for h in range(2)], axis=0)
            value = dot(value, signs[...])
            values.append(value[:32] + value[32:])
        return jnp.concatenate(values, axis=0)

    for move, groups in enumerate(MOVES):
        depth_step(move)
        for ng in range(*groups):
            time_step(ng)

    wait_rows(blocks, 15 * STEP, rsl.at[0])
    for ng in range(3):
        for r in range(8):
            q, rest = r // 2, r % 2
            if ng == 2 and rest:
                continue
            value = blocks[pl.ds(8 * ng + r, 16, stride=STEP), :]
            for half in range(2):
                n = 4 * ng + 2 * half + rest if ng < 2 else 8 + half
                for part in range(2):
                    at = 64 * half + 32 * part
                    out[part, n, q] = value[:, at : at + 32]

    wait_rows(blocks, 15 * STEP, ssl.at[0])
    for move, (first, end) in enumerate(MOVES):
        wait_rows(send_a, 63 * sent(move)[1], ssa.at[move])

        @pl.when(zero_g)
        def _():
            wait_rows(send_b, 3 * sent_b(move)[1], ssb.at[move])

        @pl.when(jnp.logical_not(zero_g))
        def _():
            wait_rows(send_b, 4 * sent_b(move)[1], ssb.at[move])

    for ng in range(3):
        wait_rows(time_send, 3 * moved(ng)[1], sst.at[ng])

        @pl.when(zero_g)
        def _():
            wait_rows(time_sb, 3 * moved(ng)[1], sstb.at[ng])

    @pl.when(zero_u)
    def _():
        wait_rows(send_a, 15 * 4, ssx.at[0])

    @pl.when(jnp.logical_not(zero_u))
    def _():
        wait_rows(send_a, 16 * 4, ssx.at[0])

    @pl.when(jnp.logical_and(zero_u, tm != 0))
    def _():
        wait_rows(time_send_x, 40, sstx.at[0])

        @pl.when(zero_g)
        def _():
            wait_rows(time_sbx, 40, sstbx.at[0])


def body(field):
    tables, at_of = all_tables()
    dma = pltpu.SemaphoreType.DMA

    def vmem(*shape):
        return pltpu.VMEM(shape, F32)

    def table(*shape):
        return pltpu.VMEM(shape, BF)

    return pl.pallas_call(
        functools.partial(kernel, at_of),
        out_shape=jax.ShapeDtypeStruct((2, CH, 4, 16, 32), F32),
        in_specs=[pl.BlockSpec(memory_space=pltpu.HBM)] * 2,
        out_specs=pl.BlockSpec(memory_space=pltpu.VMEM),
        scratch_shapes=[
            vmem(CH, 4, 4, 128, 128),
            vmem(3, 4, 512, 128), vmem(2, 128, 128),
            table(80, 256), table(160, 256), table(256, 512), table(256, 512), table(128, 256), table(128, 256),
            table(512, 256), table(512, 128), table(768, 384),
            table(512, 256), table(512, 256),
            vmem(64 * STEP, 128), vmem(48, 128), vmem(64, STEP, 128), vmem(64, 12, 128),
            vmem(320, 128), vmem(40, 128), vmem(320, 128), vmem(40, 128),
            vmem(4, 80, 128), vmem(160, 128), vmem(4, 80, 128), vmem(160, 128),
            vmem(6, 128, 128), vmem(16 * STEP, 128), vmem(16 * STEP, 128),
            dma((CH // 2,)), dma((14,)),
            dma((len(MOVES),)), dma((len(MOVES),)), dma((1,)), dma((1,)), dma((len(MOVES),)), dma((len(MOVES),)),
            dma((3,)), dma((3,)), dma((1,)), dma((1,)), dma((3,)), dma((3,)), dma((1,)), dma((1,)),
            dma((1,)), dma((1,)),
        ],
        compiler_params=pltpu.CompilerParams(
            collective_id=0, has_side_effects=True, vmem_limit_bytes=52 * 1024 * 1024
        ),
        cost_estimate=pl.CostEstimate(flops=20_000_000_000, bytes_accessed=13_000_000, transcendentals=0),
    )(field, tables)


def solution(mesh):
    return jax.shard_map(
        body,
        mesh=mesh,
        in_specs=(P(None, "tm", "space", None, None),),
        out_specs=P(None, None, "tm", "space", None),
        check_vma=False,
    )
```

profile of v0, /device:TPU:1, one launch (start us, length us, event | category | flops | bytes accessed | tf_op | source)
XLA Modules:
  0.0 43.8 jit_solution(13610658411770130934)
XLA Ops:
  0.0 43.0 %shard_map.28 = f32[2,10,4,16,32]{4,3,2,1,0:T(8,128)S(1)} custom-call(f32[10,4,4,128,128]{4,3,2,1,0:T(8,128)} %field.1, bf16[6128,256]{1,0:T(8,128)(2,1)} %constant.2.clone.tables), custom_call_target="tpu_custom_call" | custom-call | flops 20000000000 | bytes 13000000 | tf_op jit(solution)/shard_map/pallas_call | solution.py:614
  43.0 0.8 %copy.4 = f32[2,10,4,16,32]{4,3,2,1,0:T(8,128)} copy(f32[2,10,4,16,32]{4,3,2,1,0:T(8,128)S(1)} %shard_map.28) | data formatting | bytes 327680
where the time goes:
time: 43.9 us; the launch traced here: 43.8 us
  Pallas kernels  43 us (98%)
  local copies, waits for them, and re-layouts  0.84 us (2%)
    pallas_call x1, Pallas kernels, body(): pl.pallas_call(functools.partial(kernel, at_of), out_shape=jax.ShapeDtype...  43 us

commit v1 on v0

--- a/solution.py
+++ b/solution.py
@@ -28,7 +28,6 @@
     [(k // 32, (k // 8) % 4, k % 8) for k in range(1, SPACE)],
     key=lambda at: (-2 * at[0] - min(at[1], 4 - at[1]) - min(at[2], 8 - at[2]), at[1], at[2]),
 )
-PLANE_OFFSETS = [(1, 2), (1, 1), (1, 3), (1, 0), (0, 2), (0, 1), (0, 3), (0, 0)]
 TIME_AT = (0, 32, 64, 80)
 
 
@@ -234,8 +233,6 @@
         [8 * turn(place_y + d, 4) for d in range(4)],
         [turn(place_z + d, 8) for d in range(8)],
     )
-    round_z = turn(place_z, 6)
-    z_order = [turn(turn(round_z + i, 6) + 6, 8) for i in range(6)] + [4 + turn(place_z % 2 + i, 2) for i in range(2)]
     others = [along[0][x] + along[1][y] + along[2][z] for x, y, z in OFFSETS]
     for to in others:
         greet(to, tm)
@@ -323,15 +320,8 @@
         here = (s, pl.ds(first, count))
         last_move = move == len(MOVES) - 1
 
-        for z in z_order:
-            for x, y in PLANE_OFFSETS:
-                to = along[0][x] + along[1][y] + z
-                if x or y:
-                    space_copy(move, to).start()
-                else:
-                    @pl.when(to != s)
-                    def _():
-                        space_copy(move, to).start()
+        for to in others:
+            space_copy(move, to).start()
 
         if last_move:
             here_x = (s, pl.ds(20, 4))
@@ -385,8 +375,9 @@
     def wait_rows(rows_of, count, sem):
         pltpu.make_async_copy(rows_of.at[pl.ds(0, count)], rows_of.at[pl.ds(0, count)], sem).wait()
 
-    def moved(ng):
-        return TIME_AT[ng], TIME_AT[ng + 1] - TIME_AT[ng]
+    def moved(move):
+        first, end = MOVES[move]
+        return TIME_AT[first], TIME_AT[end] - TIME_AT[first]
 
     def keep_time(ng, sort, z_rows, src, src_x):
         count = (TIME_AT[ng + 1] - TIME_AT[ng]) // 2
@@ -398,17 +389,17 @@
         if ng == 2:
             src_x[...] = z_rows[64:104]
 
-    def send_time(ng, src, src_x, dst, dst_x, send_sem, recv_sem, send_sem_x, recv_sem_x):
-        first, count = moved(ng)
+    def send_time(move, src, src_x, dst, dst_x, send_sem, recv_sem, send_sem_x, recv_sem_x):
+        first, count = moved(move)
         mine = pl.ds(pl.multiple_of(tm * 80 + first, 8), count)
         here = (tm, pl.ds(first, count))
         for j in range(1, TM):
             to = tm + j
             to = jnp.where(to >= TM, to - TM, to)
             there = pl.ds(pl.multiple_of(to * 80 + first, 8), count)
-            remote(src.at[there], dst.at[here], send_sem.at[ng], recv_sem.at[ng], s, to).start()
+            remote(src.at[there], dst.at[here], send_sem.at[move], recv_sem.at[move], s, to).start()
         dst[here] = src[mine, :]
-        if ng == 2:
+        if move == len(MOVES) - 1:
             at_x = pl.ds(pl.multiple_of(tm * 40, 8), 40)
 
             @pl.when(jnp.logical_and(zero_u, tm != 0))
@@ -446,19 +437,25 @@
             def _():
                 wait_rows(send_a, 63 * 4, rsx.at[0])
 
+        z_rows = []
         for ng in range(first, end):
             both = dot(wz[...] if ng < 2 else wz2[...], received(recv_a, ng))
-            keep_time(ng, sorts.at[ng], (both[:128, :128] + both[:128, 128:] + both[128:, :128]).T, *time_a[:2])
-            send_time(ng, *time_a)
+            z_rows.append((both[:128, :128] + both[:128, 128:] + both[128:, :128]).T)
+        for ng in range(first, end):
+            keep_time(ng, sorts.at[ng], z_rows[ng - first], *time_a[:2])
+        send_time(move, *time_a)
 
         @pl.when(zero_g)
         def _():
             wait_rows(send_a, 63 * sent_b(move)[1], rsb.at[move])
+            z_rows = []
             for ng in range(first, end):
                 both = dot(wzb[...] if ng < 2 else wzb2[...], received(recv_b, ng))
-                z_rows = both[:64, :128] + both[:64, 128:] + both[64:, :128]
-                keep_time(ng, sorts.at[3 + ng], jnp.concatenate([z_rows, jnp.zeros_like(z_rows)], axis=0).T, *time_b[:2])
-                send_time(ng, *time_b)
+                both = both[:64, :128] + both[:64, 128:] + both[64:, :128]
+                z_rows.append(jnp.concatenate([both, jnp.zeros_like(both)], axis=0).T)
+            for ng in range(first, end):
+                keep_time(ng, sorts.at[3 + ng], z_rows[ng - first], *time_b[:2])
+            send_time(move, *time_b)
 
     def finish(values, table, signs):
         high, low = split(values)
@@ -492,48 +489,48 @@
         count = TIME_AT[ng + 1] - TIME_AT[ng]
         return ref[:, TIME_AT[ng] : TIME_AT[ng + 1], :].reshape(TM * count, 128)
 
-    def time_step(ng):
-        table = m01 if ng < 2 else m2
-        wait_rows(time_send, 3 * moved(ng)[1], rst.at[ng])
-        keep(ng, finish(steps_of(time_recv, ng), table, lanes), 0, False)
-        if ng == 2:
-            @pl.when(zero_e)
-            def _():
-                wait_rows(time_recv_x, 120, rstx.at[0])
-                value = finish_x(time_recv_x, lanes)
-                for i in range(3):
-                    keep(i, value[32 * i : 32 * i + 32], 4, True)
-
-        @pl.when(zero_g)
-        def _():
-            wait_rows(time_sb, 3 * moved(ng)[1], rstb.at[ng])
-            keep(ng, finish(steps_of(time_rb, ng), table, lanes_b), 0, True)
-            if ng == 2:
+    def time_step(move):
+        first, end = MOVES[move]
+        rows_at, rows_count = 8 * first, 8 * (end - first)
+
+        def finish_all(ref, ref_x, signs, recv_sem_x, add):
+            values = [finish(steps_of(ref, ng), m01 if ng < 2 else m2, signs) for ng in range(first, end)]
+            for ng in range(first, end):
+                keep(ng, values[ng - first], 0, add)
+            if end == 3:
                 @pl.when(zero_e)
                 def _():
-                    wait_rows(time_rbx, 120, rstbx.at[0])
-                    value = finish_x(time_rbx, lanes_b)
+                    wait_rows(time_recv_x, 120, recv_sem_x.at[0])
+                    value = finish_x(ref_x, signs)
                     for i in range(3):
                         keep(i, value[32 * i : 32 * i + 32], 4, True)
 
+        wait_rows(time_send, 3 * moved(move)[1], rst.at[move])
+        finish_all(time_recv, time_recv_x, lanes, rstx, False)
+
+        @pl.when(zero_g)
+        def _():
+            wait_rows(time_sb, 3 * moved(move)[1], rstb.at[move])
+            finish_all(time_rb, time_rbx, lanes_b, rstbx, True)
+
         @pl.when(jnp.logical_not(zero_e))
         def _():
             side = jnp.where(e >= 8, 8, 0)
             for k in range(8):
-                last_copy(8 - side + k, 8 * ng, 8).start()
+                last_copy(8 - side + k, rows_at, rows_count).start()
             for k in range(1, 8):
-                last_copy(side + turn(e - side + k, 8), 8 * ng, 8).start()
+                last_copy(side + turn(e - side + k, 8), rows_at, rows_count).start()
 
         @pl.when(zero_e)
         def _():
             for j in (8, 9, 10, 11, 1, 2, 3):
-                last_copy(j, 8 * ng, 8).start()
-            if ng == 2:
+                last_copy(j, rows_at, rows_count).start()
+            if end == 3:
                 for j in (12, 13, 14, 15, 4, 5, 6, 7):
                     last_copy(j, 0, STEP).start()
 
-        at = pl.ds(pl.multiple_of(slot_of(u % 2) * STEP + 8 * ng, 8), 8)
-        blocks[at, :] = last[pl.ds(pl.multiple_of(e * STEP + 8 * ng, 8), 8), :]
+        at = pl.ds(pl.multiple_of(slot_of(u % 2) * STEP + rows_at, 8), rows_count)
+        blocks[at, :] = last[pl.ds(pl.multiple_of(e * STEP + rows_at, 8), rows_count), :]
 
     def finish_x(ref, signs):
         high, low = split(ref[...])
@@ -547,10 +544,9 @@
             values.append(value[:32] + value[32:])
         return jnp.concatenate(values, axis=0)
 
-    for move, groups in enumerate(MOVES):
+    for move in range(len(MOVES)):
         depth_step(move)
-        for ng in range(*groups):
-            time_step(ng)
+        time_step(move)
 
     wait_rows(blocks, 15 * STEP, rsl.at[0])
     for ng in range(3):
@@ -577,12 +573,12 @@
         def _():
             wait_rows(send_b, 4 * sent_b(move)[1], ssb.at[move])
 
-    for ng in range(3):
-        wait_rows(time_send, 3 * moved(ng)[1], sst.at[ng])
+    for move in range(len(MOVES)):
+        wait_rows(time_send, 3 * moved(move)[1], sst.at[move])
 
         @pl.when(zero_g)
         def _():
-            wait_rows(time_sb, 3 * moved(ng)[1], sstb.at[ng])
+            wait_rows(time_sb, 3 * moved(move)[1], sstb.at[move])
 
     @pl.when(zero_u)
     def _():
@@ -628,7 +624,8 @@
             vmem(6, 128, 128), vmem(16 * STEP, 128), vmem(16 * STEP, 128),
             dma((CH // 2,)), dma((14,)),
             dma((len(MOVES),)), dma((len(MOVES),)), dma((1,)), dma((1,)), dma((len(MOVES),)), dma((len(MOVES),)),
-            dma((3,)), dma((3,)), dma((1,)), dma((1,)), dma((3,)), dma((3,)), dma((1,)), dma((1,)),
+            dma((len(MOVES),)), dma((len(MOVES),)), dma((1,)), dma((1,)),
+            dma((len(MOVES),)), dma((len(MOVES),)), dma((1,)), dma((1,)),
             dma((1,)), dma((1,)),
         ],
         compiler_params=pltpu.CompilerParams(

time: 43.9 us -> 43.6 us (level)
  no operation moved by 1% of the time
where the time goes in v1:
time: 43.6 us
  Pallas kernels  42.7 us (98%)
  local copies, waits for them, and re-layouts  0.84 us (2%)
    pallas_call x1, Pallas kernels, body(): pl.pallas_call(functools.partial(kernel, at_of), out_shape=jax.ShapeDtype...  42.7 us

profile of v1, /device:TPU:1, one launch (start us, length us, event | category | flops | bytes accessed | tf_op | source)
XLA Modules:
  0.0 43.6 jit_solution(194850820091300511)
XLA Ops:
  0.0 42.7 %shard_map.28 = f32[2,10,4,16,32]{4,3,2,1,0:T(8,128)S(1)} custom-call(f32[10,4,4,128,128]{4,3,2,1,0:T(8,128)} %field.1, bf16[6128,256]{1,0:T(8,128)(2,1)} %constant.2.clone.tables), custom_call_target="tpu_custom_call" | custom-call | flops 20000000000 | bytes 13000000 | tf_op jit(solution)/shard_map/pallas_call | solution.py:610
  42.7 0.8 %copy.4 = f32[2,10,4,16,32]{4,3,2,1,0:T(8,128)} copy(f32[2,10,4,16,32]{4,3,2,1,0:T(8,128)S(1)} %shard_map.28) | data formatting | bytes 327680

commit v2 on v1

--- a/solution.py
+++ b/solution.py
@@ -163,6 +163,12 @@
     return high, (values - high.astype(F32)).astype(BF)
 
 
+def split_wide(values):
+    scaled = values * 65537.0
+    high = scaled - (scaled - values)
+    return high, values - high
+
+
 def dot(a, b):
     return jnp.dot(a, b, preferred_element_type=F32)
 
@@ -251,11 +257,12 @@
     send_b[...] = jnp.zeros_like(send_b)
 
     def plane_step(ng, first, n):
+        wx_wide = wx[...].astype(F32)
         products = []
         for t in range(4):
             for pair in range(2):
-                high, low = split(jnp.concatenate([planes[n, t, 2 * pair], planes[n, t, 2 * pair + 1]], axis=1))
-                both = dot(wx[...], jnp.concatenate([high, low], axis=0))
+                high, low = split_wide(jnp.concatenate([planes[n, t, 2 * pair], planes[n, t, 2 * pair + 1]], axis=1))
+                both = dot(wx_wide, jnp.concatenate([high, low], axis=0))
                 products.append((t, pair, both[:40] + both[40:]))
         for t, pair, both in products:
             at = pl.multiple_of(((n - first) * 4 + t) * 8, 8)

time: 43.6 us -> 43.7 us (level)
  no operation moved by 1% of the time
where the time goes in v2:
time: 43.7 us
  Pallas kernels  42.8 us (98%)
  local copies, waits for them, and re-layouts  0.84 us (2%)
    pallas_call x1, Pallas kernels, body(): pl.pallas_call(functools.partial(kernel, at_of), out_shape=jax.ShapeDtype...  42.8 us

profile of v2, /device:TPU:1, one launch (start us, length us, event | category | flops | bytes accessed | tf_op | source)
XLA Modules:
  0.0 43.7 jit_solution(12019293893990956207)
XLA Ops:
  0.0 42.8 %shard_map.28 = f32[2,10,4,16,32]{4,3,2,1,0:T(8,128)S(1)} custom-call(f32[10,4,4,128,128]{4,3,2,1,0:T(8,128)} %field.1, bf16[6128,256]{1,0:T(8,128)(2,1)} %constant.2.clone.tables), custom_call_target="tpu_custom_call" | custom-call | flops 20000000000 | bytes 13000000 | tf_op jit(solution)/shard_map/pallas_call | solution.py:617
  42.8 0.8 %copy.4 = f32[2,10,4,16,32]{4,3,2,1,0:T(8,128)} copy(f32[2,10,4,16,32]{4,3,2,1,0:T(8,128)S(1)} %shard_map.28) | data formatting | bytes 327680

commit v3 on v2

--- a/solution.py
+++ b/solution.py
@@ -26,7 +26,7 @@
 MOVES = ((0, 1), (1, 3))
 OFFSETS = sorted(
     [(k // 32, (k // 8) % 4, k % 8) for k in range(1, SPACE)],
-    key=lambda at: (-2 * at[0] - min(at[1], 4 - at[1]) - min(at[2], 8 - at[2]), at[1], at[2]),
+    key=lambda at: (-min(at[1], 4 - at[1]) - min(at[2], 8 - at[2]), at[1], at[2], at[0]),
 )
 TIME_AT = (0, 32, 64, 80)
 
@@ -476,9 +476,9 @@
         both = dot(both, signs[...])
         return both[:count] + both[count:]
 
-    def keep(ng, value, first, add):
+    def keep(ng, value, first, add, sides):
         for i in range(value.shape[0] // 8):
-            for sy in range(2):
+            for sy in sides:
                 j = 8 * sy + first + i
                 part = value[8 * i : 8 * i + 8, 128 * sy : 128 * sy + 128]
                 at = slice(j * STEP + 8 * ng, j * STEP + 8 * ng + 8)
@@ -500,41 +500,63 @@
         first, end = MOVES[move]
         rows_at, rows_count = 8 * first, 8 * (end - first)
 
-        def finish_all(ref, ref_x, signs, recv_sem_x, add):
+        def finish_all(ref, ref_x, signs, recv_sem_x, add, sides):
             values = [finish(steps_of(ref, ng), m01 if ng < 2 else m2, signs) for ng in range(first, end)]
             for ng in range(first, end):
-                keep(ng, values[ng - first], 0, add)
+                keep(ng, values[ng - first], 0, add, sides)
             if end == 3:
                 @pl.when(zero_e)
                 def _():
                     wait_rows(time_recv_x, 120, recv_sem_x.at[0])
                     value = finish_x(ref_x, signs)
                     for i in range(3):
-                        keep(i, value[32 * i : 32 * i + 32], 4, True)
+                        keep(i, value[32 * i : 32 * i + 32], 4, True, sides)
 
         wait_rows(time_send, 3 * moved(move)[1], rst.at[move])
-        finish_all(time_recv, time_recv_x, lanes, rstx, False)
+        finish_all(time_recv, time_recv_x, lanes, rstx, False, (0, 1))
+
+        def send_side(side):
+            @pl.when(jnp.logical_and(jnp.logical_not(zero_e), (e >= 8) == (side == 1)))
+            def _():
+                for k in range(1, 8):
+                    last_copy(8 * side + turn(e - 8 * side + k, 8), rows_at, rows_count).start()
+
+            @pl.when((e >= 8) != (side == 1))
+            def _():
+                for k in range(8):
+                    if side == 0 or k < 4:
+                        last_copy(8 * side + k, rows_at, rows_count).start()
+                if side == 1:
+                    @pl.when(jnp.logical_not(zero_e))
+                    def _():
+                        for k in range(4, 8):
+                            last_copy(8 + k, rows_at, rows_count).start()
+
+            @pl.when(zero_e)
+            def _():
+                if side == 0:
+                    for j in range(1, 4):
+                        last_copy(j, rows_at, rows_count).start()
+                if end == 3:
+                    for j in range(8 * side + 4, 8 * side + 8):
+                        last_copy(j, 0, STEP).start()
 
         @pl.when(zero_g)
         def _():
+            send_side(0)
             wait_rows(time_sb, 3 * moved(move)[1], rstb.at[move])
-            finish_all(time_rb, time_rbx, lanes_b, rstbx, True)
-
-        @pl.when(jnp.logical_not(zero_e))
-        def _():
-            side = jnp.where(e >= 8, 8, 0)
-            for k in range(8):
-                last_copy(8 - side + k, rows_at, rows_count).start()
-            for k in range(1, 8):
-                last_copy(side + turn(e - side + k, 8), rows_at, rows_count).start()
-
-        @pl.when(zero_e)
-        def _():
-            for j in (8, 9, 10, 11, 1, 2, 3):
-                last_copy(j, rows_at, rows_count).start()
-            if end == 3:
-                for j in (12, 13, 14, 15, 4, 5, 6, 7):
-                    last_copy(j, 0, STEP).start()
+            finish_all(time_rb, time_rbx, lanes_b, rstbx, True, (1,))
+            send_side(1)
+
+        @pl.when(jnp.logical_and(jnp.logical_not(zero_g), e < 8))
+        def _():
+            send_side(1)
+            send_side(0)
+
+        @pl.when(jnp.logical_and(jnp.logical_not(zero_g), e >= 8))
+        def _():
+            send_side(0)
+            send_side(1)
 
         at = pl.ds(pl.multiple_of(slot_of(u % 2) * STEP + rows_at, 8), rows_count)
         blocks[at, :] = last[pl.ds(pl.multiple_of(e * STEP + rows_at, 8), rows_count), :]

time: 43.7 us -> 43.3 us (level)
  the two profiles are of different devices: /device:TPU:1 before, /device:TPU:71 now
where the time goes in v3:
time: 43.3 us; the launch traced here: 43.2 us
  Pallas kernels  42.4 us (98%)
  local copies, waits for them, and re-layouts  0.84 us (2%)
    pallas_call x1, Pallas kernels, body(): pl.pallas_call(functools.partial(kernel, at_of), out_shape=jax.ShapeDtype...  42.4 us

profile of v3, /device:TPU:71, one launch (start us, length us, event | category | flops | bytes accessed | tf_op | source)
XLA Modules:
  0.0 43.2 jit_solution(14248959975280044307)
XLA Ops:
  0.0 42.4 %shard_map.28 = f32[2,10,4,16,32]{4,3,2,1,0:T(8,128)S(1)} custom-call(f32[10,4,4,128,128]{4,3,2,1,0:T(8,128)} %field.1, bf16[6128,256]{1,0:T(8,128)(2,1)} %constant.2.clone.tables), custom_call_target="tpu_custom_call" | custom-call | flops 20000000000 | bytes 13000000 | tf_op jit(solution)/shard_map/pallas_call | solution.py:639
  42.4 0.8 %copy.4 = f32[2,10,4,16,32]{4,3,2,1,0:T(8,128)} copy(f32[2,10,4,16,32]{4,3,2,1,0:T(8,128)S(1)} %shard_map.28) | data formatting | bytes 327680
